TPU v7x, 256 devices: a whole 4x4x8 slice. The times are simulated.
256 devices in a mesh: boot: 8 (over z), tm: 32 (over x, y, core).
Axes of the slice: x: 4, y: 4, z: 8, core: 2. Of those that a mesh axis runs over, the one named last changes fastest.
Arguments:
- recording: bfloat16 [16384, 1024], P('tm'), may hold values from -60 to 60, as said below
- starts: int32 [8, 192], P('boot', 'tm'), may hold values from 0 to 448, as said below
- lengths: int32 [8, 192], P('boot', 'tm'), may hold values from 1 to 64, as said below
- support: int32 [8, 4096], P(None, 'boot'), may hold values 0 or 1
Outputs:
- averaged: float32 [32, 4096], P(None, 'boot')
- residual: float32 [32, 16384], P(None, 'tm')
Inputs may be any that keep to these rules, and one draw needn't show every extreme that they name: A shard's values are an autoregressive recording; its values stay within the range. Entry [b, j * 6 + k] starts block k of resample b on time shard j, counted from the shard's first sample; a block ends inside its shard. The 6 lengths of one resample on one time shard sum to at most 384.
All inputs are finite; a program needn't handle non-finite values. No bound on the sum of `support` on one device may be relied on, other than what follows from the above.
Results may differ from a plain program's by a relative error of at most 0.0043.
The roundings to bfloat16 on the way count: a program that leaves them out, or rounds other values in their place, can miss the bound.
Values may be sent and summed in bfloat16 or wider, within the bound.
A program may use at most 64 MiB of HBM per device.

v0:
```python
import jax
import jax.numpy as jnp
from jax import lax
from jax.sharding import PartitionSpec as P

CHANNEL_COUNT = 1024
LAGS = 4
RESPONSE_COUNT = 32
NBLK = 6
CAP = 384
ITERS = 3
CHEB = 5


ridge_weight = 4.0
shrink_level = 0.75
epsilon = 1e-05


def passed_along(block, axis, distance):
    devices = range(lax.axis_size(axis))
    route = [(i - distance, i) for i in devices if i - distance in devices]
    return lax.ppermute(block, axis, route)


def bootstrap_rows(window, begins, sizes):
    ends = jnp.cumsum(sizes)
    offsets = ends - sizes
    total = ends[-1]
    rows = jnp.arange(CAP, dtype=jnp.int32)
    member = (rows[:, None] >= offsets[None, :]).astype(jnp.int32)
    which = jnp.sum(member, axis=1) - 1
    picked = (which[:, None] == jnp.arange(NBLK, dtype=jnp.int32)[None, :]).astype(jnp.int32)
    anchor = jnp.sum(picked * offsets[None, :], axis=1)
    opening = jnp.sum(picked * begins[None, :], axis=1)
    live = rows < total
    times = jnp.where(live, opening + rows - anchor, 0)
    blocks = [jnp.take(window, times + LAGS - 1 - delay_step, axis=0) for delay_step in range(LAGS)]
    design = jnp.concatenate(blocks, axis=1)
    design = jnp.where(live[:, None], design, jnp.zeros_like(design))
    answer = jnp.take(window[:, :RESPONSE_COUNT], times + LAGS, axis=0)
    answer = jnp.where(live[:, None], answer, jnp.zeros_like(answer))
    return (design, answer.T)


def chebyshev(gram, rhs, bound):
    center = ridge_weight + 0.5 * bound
    radius = 0.5 * bound
    sigma = center / radius
    solution = jnp.zeros_like(rhs)
    remain = rhs
    factor = 1.0 / sigma
    update = rhs / center
    for count in range(CHEB):
        solution = solution + update
        if count + 1 < CHEB:
            applied = ridge_weight * update + jnp.einsum(
                "brc,bcd->brd", update, gram, precision=lax.Precision.HIGHEST
            )
            remain = remain - applied
            after = 1.0 / (2.0 * sigma - factor)
            update = after * factor * update + 2.0 * after / radius * remain
            factor = after
    return solution


def shrink_columns(mean_value, norms, level):
    return mean_value * (jnp.maximum(norms - level, 0.0) / jnp.maximum(norms, level))[:, None, :]


def per_device(recording, starts, lengths, support):
    shards = lax.axis_size("tm")
    samples = recording.shape[0]
    values = recording.astype(jnp.float32)
    power = lax.psum(jnp.sum(values * values, axis=0), "tm")
    scale = 1.0 / jnp.sqrt(power / (samples * shards) + epsilon)
    scaled_input = (values * scale).astype(jnp.bfloat16)
    carried = passed_along(scaled_input[samples - LAGS :], "tm", 1)
    extended = jnp.concatenate([carried, scaled_input], axis=0)
    design, answer = jax.vmap(bootstrap_rows, in_axes=(None, 0, 0))(extended, starts, lengths)
    row_scale = 1.0 / CAP
    cross = (
        jnp.einsum("brc,bcf->brf", answer, design, preferred_element_type=jnp.float32) * row_scale
    )
    gram = (
        jnp.einsum("bcf,bdf->bcd", design, design, preferred_element_type=jnp.float32) * row_scale
    )
    bound = jnp.sqrt(jnp.sum(gram * gram, axis=(1, 2)))[:, None, None]
    consensus = jnp.zeros_like(cross)
    dual = jnp.zeros_like(cross)
    for rounds in range(ITERS):
        target = cross + ridge_weight * (consensus - dual)
        projected = (
            jnp.einsum(
                "brf,bcf->brc",
                target.astype(jnp.bfloat16),
                design,
                preferred_element_type=jnp.float32,
            )
            * row_scale
        )
        weights = chebyshev(gram, projected, bound)
        back = jnp.einsum(
            "brc,bcf->brf", weights.astype(jnp.bfloat16), design, preferred_element_type=jnp.float32
        )
        local = (target - back) / ridge_weight
        stacked = local + dual
        mean_value = lax.psum(stacked, "tm") / shards
        norms = jnp.sqrt(jnp.sum(mean_value * mean_value, axis=1))
        level = shrink_level * jnp.mean(norms, axis=1, keepdims=True)
        consensus = shrink_columns(mean_value, norms, level)
        dual = dual + local - consensus
    width = consensus.shape[2] // lax.axis_size("boot")
    position = lax.axis_index("boot")
    chosen = support.astype(jnp.float32)
    tally = jnp.sum(chosen, axis=0)
    everything = lax.all_gather(consensus, "boot", axis=0, tiled=True)
    grouped = lax.dynamic_slice_in_dim(everything, position * width, width, 2)
    averaged = jnp.sum(chosen[:, None, :] * grouped, axis=0) / jnp.maximum(tally, 1.0)[None, :]
    opening = position * width
    delay_step = opening // CHANNEL_COUNT
    channel = opening % CHANNEL_COUNT
    columns = lax.dynamic_slice(extended, (LAGS - 1 - delay_step, channel), (samples, width))
    partial_result = lax.dot_general(
        averaged.astype(jnp.bfloat16),
        columns,
        (((1,), (1,)), ((), ())),
        preferred_element_type=jnp.float32,
    )
    predicted_output = lax.psum(partial_result, "boot")
    residual = scaled_input[:, :RESPONSE_COUNT].astype(jnp.float32).T - predicted_output
    return (averaged, residual)


def solution(mesh):
    in_specs = (P("tm", None), P("boot", "tm"), P("boot", "tm"), P(None, "boot"))
    out_specs = (P(None, "boot"), P(None, "tm"))
    return jax.shard_map(
        per_device, mesh=mesh, in_specs=in_specs, out_specs=out_specs, check_vma=False
    )
```

profile of v0, /device:TPU:1, one launch (start us, length us, event | category | flops | bytes accessed | tf_op | source)
XLA Modules:
  0.0 605.6 jit_solution(16452288002245267137)
XLA Ops:
  7.2 1.5 copy.24
  9.0 65.3 %psum.35 = f32[1024]{0:T(1024)S(1)} all-reduce(f32[1024]{0:T(1024)S(1)} %fusion.9), channel_id=1, replica_groups=mesh['boot'=8,'tm'=32] {'tm'}, use_global_device_ids=true, to_apply=%region_5.6 | all-reduce | flops 1024 | bytes 8192 | tf_op jit(solution)/shard_map/psum | solution.py:75
  74.7 1.9 collective-permute-start
  76.9 0.6 slice.12
  77.7 0.7 iota_compare_fusion
  78.3 0.7 fusion.114
  79.0 0.7 and_reduce_fusion.3
  79.8 0.8 collective-permute-done
  80.6 0.7 copy-done.10
  81.3 0.7 pad_maximum_fusion
  82.0 0.6 copy.26
  82.6 2.7 gather_fusion.4
  85.3 2.7 gather_fusion.3
  88.0 2.7 gather_fusion.2
  90.7 2.7 gather_fusion.1
  93.4 2.7 fusion.38
  96.1 1.4 fusion.42
  97.5 0.9 fusion.8
  98.4 2.5 multiply_reduce_fusion
  102.2 1.4 gather_fusion
  103.6 2.7 convolution_multiply_fusion
  106.3 2.1 maximum_select_fusion.1
  108.4 1.0 convolution_multiply_fusion.4
  110.4 0.4 fusion.29
  110.8 0.5 fusion.32
  111.3 1.5 fusion.1
  113.0 112.8 %all-reduce.5.cloned.1.call-done = f32[1,32,4096]{2,1,0:T(8,128)} async-done(((f32[1,32,4096]{2,1,0:T(8,128)}), f32[1,32,4096]{2,1,0:T(8,128)}) %all-reduce.5.cloned.1.call-update) | async-done | bytes 524304 | tf_op jit(solution)/shard_map/psum | solution.py:108
  225.8 1.1 multiply_reduce_fusion.4
  227.0 0.7 sqrt_reduce_fusion.2
  228.3 3.4 convolution_multiply_fusion.3
  232.6 0.4 fusion.22
  233.0 0.5 fusion.33
  233.5 1.5 fusion.7
  235.2 113.2 %all-reduce.7.cloned.1.call-done = f32[1,32,4096]{2,1,0:T(8,128)} async-done(((f32[1,32,4096]{2,1,0:T(8,128)}), f32[1,32,4096]{2,1,0:T(8,128)}) %all-reduce.7.cloned.1.call-update) | async-done | bytes 524304 | tf_op jit(solution)/shard_map/psum | solution.py:108
  348.4 1.1 multiply_reduce_fusion.3
  349.5 0.7 sqrt_reduce_fusion.1
  350.9 3.4 convolution_multiply_fusion.2
  355.6 0.5 fusion.34
  356.1 1.5 fusion.4
  357.7 113.2 %all-reduce.9.cloned.1.call-done = f32[1,32,4096]{2,1,0:T(8,128)} async-done(((f32[1,32,4096]{2,1,0:T(8,128)}), f32[1,32,4096]{2,1,0:T(8,128)}) %all-reduce.9.cloned.1.call-update) | async-done | bytes 524304 | tf_op jit(solution)/shard_map/psum | solution.py:108
  470.9 1.1 multiply_reduce_fusion.2
  472.0 0.6 sqrt_reduce_fusion
  473.3 1.9 broadcast_multiply_fusion
  475.4 54.4 %all-gather.2.cloned.1.call-done = f32[8,32,4096]{2,1,0:T(8,128)} async-done(((f32[1,32,4096]{2,1,0:T(8,128)}), f32[8,32,4096]{2,1,0:T(8,128)}) %all-gather.2.cloned.1.call-update) | async-done | bytes 4194320 | tf_op jit(solution)/shard_map/all_gather | solution.py:117
  529.8 1.1 multiply_reduce_fusion.1
  530.9 1.1 fusion.36
  532.1 65.5 %all-reduce.11.cloned.1.call-done = f32[32,512]{1,0:T(8,128)} async-done(((f32[32,512]{1,0:T(8,128)}), f32[32,512]{1,0:T(8,128)}) %all-reduce.11.cloned.1.call-update) | async-done | bytes 65552 | tf_op jit(solution)/shard_map/psum | solution.py:130
  597.6 1.5 bitcast_subtract_fusion
  (72 shorter events, 5.0 us)
Async XLA Ops:
  7.2 69.5 %copy-start.15 = (s32[1,6]{1,0:T(1,128)S(1)}, s32[1,6]{1,0:T(1,128)}, u32[]{:S(2)}) copy-start(s32[1,6]{1,0:T(1,128)} %param.8) | copy-start | bytes 76
  7.2 70.4 %copy-start.14 = (s32[1,6]{1,0:T(1,128)S(1)}, s32[1,6]{1,0:T(1,128)}, u32[]{:S(2)}) copy-start(s32[1,6]{1,0:T(1,128)} %param.7) | copy-start | bytes 76
  7.2 218.7 %all-reduce.5.cloned.1.call-start = ((), (), s32[]{:S(2)}) async-start(), calls=%async_computation | async-start | bytes 1048576 | tf_op jit(solution)/shard_map/psum | solution.py:108
  74.7 5.9 collective-permute-start
  80.6 0.7 copy-start.10
  93.4 2.7 copy-start.8
  93.4 2.7 copy-start.9
  98.3 2.5 copy-start.3
  98.4 3.4 copy-start.11
  108.4 2.8 copy-start
  112.8 235.6 %all-reduce.7.cloned.1.call-start = ((), (), s32[]{:S(2)}) async-start(), calls=%async_computation.1 | async-start | bytes 1048576 | tf_op jit(solution)/shard_map/psum | solution.py:108
  228.3 5.2 copy-start.1
  228.3 5.2 copy-start.5
  228.3 5.2 copy-start.7
  235.1 235.8 %all-reduce.9.cloned.1.call-start = ((), (), s32[]{:S(2)}) async-start(), calls=%async_computation.2 | async-start | bytes 1048576 | tf_op jit(solution)/shard_map/psum | solution.py:108
  350.8 5.2 copy-start.2
  350.8 5.2 copy-start.4
  350.8 5.2 copy-start.6
  356.1 119.2 %copy-start.13 = (s32[8,512]{1,0:T(8,128)S(1)}, s32[8,512]{1,0:T(8,128)}, u32[]{:S(2)}) copy-start(s32[8,512]{1,0:T(8,128)} %param.9) | copy-start | bytes 49156
  357.6 172.2 %all-gather.2.cloned.1.call-start = ((), (), s32[]{:S(2)}) async-start(), calls=%async_computation.3 | async-start | bytes 4718592 | tf_op jit(solution)/shard_map/all_gather | solution.py:117
  475.2 122.4 %all-reduce.11.cloned.1.call-start = ((), (), s32[]{:S(2)}) async-start(), calls=%async_computation.4 | async-start | bytes 131072 | tf_op jit(solution)/shard_map/psum | solution.py:130
  530.9 68.2 %copy-start.12 = (f32[32,512]{1,0:T(8,128)}, f32[32,512]{1,0:T(8,128)S(1)}, u32[]{:S(2)}) copy-start(f32[32,512]{1,0:T(8,128)S(1)} %broadcast_divide_fusion) | copy-start | bytes 196612
Sparse Core Ops, SparseCore 0:
  112.9 112.8 all-reduce.4
  235.2 113.1 all-reduce.6
  357.8 113.0 all-reduce.8
  475.3 54.4 all-gather.1
  532.6 64.9 all-reduce.10
where the time goes:
time: 610 us; the launch traced here: 606 us
  waiting for transfers between devices  460 us (75%)
  blocking collectives  65.3 us (11%)
  matrix products  23.9 us (4%)
  other arithmetic  20.7 us (3%)
  between operations  17.4 us (3%)
  local copies, waits for them, and re-layouts  15.9 us (3%)
    psum x3, waiting for transfers between devices, per_device(): mean_value = lax.psum(stacked, 'tm') / shards  339 us
    psum x1, waiting for transfers between devices, per_device(): predicted_output = lax.psum(partial_result, 'boot')  65.5 us
    psum x1, blocking collectives, per_device(): power = lax.psum(jnp.sum(values * values, axis=0), 'tm')  65.3 us
    all_gather x1, waiting for transfers between devices, per_device(): everything = lax.all_gather(consensus, 'boot', axis=0, tiled=True)  54.4 us
  transfers between devices with their start and end apart: 6, of which 6 were waited for; matrix products, arithmetic and copies ran while one was open for 1% of the time, Pallas kernels for 0%

commit v1 on v0

v1 whole, which is shorter than its diff:
```python
import functools

import jax
import jax.numpy as jnp
from jax import lax
from jax.experimental import pallas as pl
from jax.experimental.pallas import tpu as pltpu
from jax.sharding import PartitionSpec as P

CHANNELS = 1024
LAGS = 4
FEAT = LAGS * CHANNELS
RESP = 32
NBLK = 6
CAP = 384
SEG = 512
ITERS = 3
CHEB = 5
HEAD = 16
WINDOW = 640
CHUNK = 128

RHO = 4.0
SHRINK = 0.75
EPSILON = 1e-05

HIGHEST = lax.Precision.HIGHEST
NT = (((1,), (1,)), ((), ()))
HALO, POWER, SUPPORT, SCATTER, GATHER, NORMS, BOOTS, FINAL = 0, 1, 2, 3, 6, 8, 9, 10
PHASES = 11


def chebyshev_terms(bound):
    theta = RHO + 0.5 * bound
    delta = 0.5 * bound
    sigma = theta / delta
    nought = jnp.zeros_like(bound)
    total = [nought] * CHEB
    remain = [jnp.ones_like(bound)] + [nought] * (CHEB - 1)
    factor = 1.0 / sigma
    update = [term / theta for term in remain]
    for count in range(CHEB):
        total = [a + b for a, b in zip(total, update)]
        if count + 1 < CHEB:
            applied = [
                theta * update[k] + (delta * update[k - 1] if k else 0.0)
                for k in range(CHEB)
            ]
            remain = [a - b for a, b in zip(remain, applied)]
            after = 1.0 / (2.0 * sigma - factor)
            update = [
                after * factor * d + 2.0 * after / delta * r
                for d, r in zip(update, remain)
            ]
            factor = after
    return total, delta


def kernel(
    tm,
    boots,
    rec_ref,
    starts_ref,
    lengths_ref,
    support_ref,
    avg_ref,
    res_ref,
    halo,
    power,
    sup,
    ext,
    design,
    cross,
    v,
    z,
    tb,
    outgoing,
    incoming,
    gathered,
    norms,
    zx,
    final,
    send_sem,
    recv_sem,
):
    b = lax.axis_index("boot")
    me = lax.axis_index("tm")

    def tm_peer(i):
        return lax.rem(me + i, tm)

    def boot_peer(i):
        return lax.rem(b + i, boots)

    barrier = pltpu.get_barrier_semaphore()

    @pl.loop(1, tm)
    def _(i):
        pl.semaphore_signal(
            barrier, inc=1, device_id={"tm": tm_peer(i)}, device_id_type=pl.DeviceIdType.MESH
        )

    @pl.loop(1, boots)
    def _(i):
        pl.semaphore_signal(
            barrier, inc=1, device_id={"boot": boot_peer(i)}, device_id_type=pl.DeviceIdType.MESH
        )

    def send(src, dst, phase, target):
        pltpu.make_async_remote_copy(
            src_ref=src,
            dst_ref=dst,
            send_sem=send_sem.at[phase],
            recv_sem=recv_sem.at[phase],
            device_id=target,
            device_id_type=pl.DeviceIdType.MESH,
        ).start()

    def to_tm(src, dst, phase):
        @pl.loop(1, tm)
        def _(i):
            send(src, dst, phase, {"tm": tm_peer(i)})

    def to_boots(src, dst, phase):
        @pl.loop(1, boots)
        def _(i):
            send(src, dst, phase, {"boot": boot_peer(i)})

    def arrived(ref, phase):
        pltpu.make_async_copy(ref, ref, recv_sem.at[phase]).wait()

    def left(ref, phase):
        pltpu.make_async_copy(ref, ref, send_sem.at[phase]).wait()

    acc = jnp.zeros((8, CHANNELS), jnp.float32)

    def add_rows(k, acc):
        block = rec_ref[pl.ds(pl.multiple_of(k * 16, 16), 16), :].astype(jnp.float32)
        block = block * block
        return acc + block[:8] + block[8:]

    acc = lax.fori_loop(0, SEG // 16, add_rows, acc)
    power[me] = jnp.sum(acc, axis=0, keepdims=True)

    pl.semaphore_wait(barrier, tm + boots - 2)
    to_tm(power.at[me], power.at[me], POWER)
    send(rec_ref.at[pl.ds(SEG - HEAD, HEAD)], halo, HALO, {"tm": tm_peer(1)})
    to_boots(support_ref, sup.at[b], SUPPORT)
    sup[b] = support_ref[...]

    row = lax.broadcasted_iota(jnp.int32, (CAP, CHUNK), 0)
    place = jnp.full((CAP, CHUNK), -4 * WINDOW, jnp.int32)
    offset = jnp.int32(0)
    for k in range(NBLK):
        length = lengths_ref[0, k]
        inside = (row >= offset) & (row < offset + length)
        place = jnp.where(inside, row + (starts_ref[0, k] - offset + HEAD), place)
        offset = offset + length
    lane = lax.broadcasted_iota(jnp.int32, (CAP, CHUNK), 1)

    def picks(back):
        return jnp.concatenate(
            [
                jnp.where(place - back == lane + c * CHUNK, 1.0, 0.0).astype(jnp.bfloat16)
                for c in range(WINDOW // CHUNK)
            ],
            axis=1,
        )

    arrived(power.at[pl.ds(0, tm - 1)], POWER)
    total = jnp.sum(power[...], axis=0)
    scale = 1.0 / jnp.sqrt(total / (SEG * tm) + EPSILON)

    def scale_rows(k, carry):
        at = pl.multiple_of(k * 16, 16)
        block = rec_ref[pl.ds(at, 16), :].astype(jnp.float32) * scale
        ext[pl.ds(pl.multiple_of(at + HEAD, 16), 16), :] = block.astype(jnp.bfloat16)
        return carry

    lax.fori_loop(0, SEG // 16, scale_rows, 0)
    arrived(halo, HALO)
    first = (halo[...].astype(jnp.float32) * scale).astype(jnp.bfloat16)
    ext[0:HEAD, :] = jnp.where(me == 0, jnp.zeros_like(first), first)
    ext[HEAD + SEG :, :] = jnp.zeros((WINDOW - HEAD - SEG, CHANNELS), jnp.bfloat16)

    answer = jnp.dot(picks(0), ext[:, :CHUNK], preferred_element_type=jnp.float32)
    answer = jnp.transpose(answer)[:RESP].astype(jnp.bfloat16)
    gram = jnp.zeros((CAP, CAP), jnp.float32)
    for lag in range(LAGS):
        pick = picks(1 + lag)
        for part in range(4):
            at = lag * CHANNELS + part * 256
            block = jnp.dot(
                pick, ext[:, part * 256 : (part + 1) * 256], preferred_element_type=jnp.float32
            ).astype(jnp.bfloat16)
            design[:, at : at + 256] = block
            fit = jnp.dot(answer, block, preferred_element_type=jnp.float32) * (1.0 / CAP)
            cross[:, at : at + 256] = fit
            tb[:, at : at + 256] = fit.astype(jnp.bfloat16)
        piece = design[:, lag * CHANNELS : (lag + 1) * CHANNELS]
        gram = gram + lax.dot_general(piece, piece, NT, preferred_element_type=jnp.float32)
    gram = gram * (1.0 / CAP)
    bound = jnp.sqrt(jnp.sum(jnp.sum(gram * gram, axis=1, keepdims=True), axis=0, keepdims=True))
    terms, delta = chebyshev_terms(bound)
    ri = lax.broadcasted_iota(jnp.int32, (CAP, CAP), 0)
    ci = lax.broadcasted_iota(jnp.int32, (CAP, CAP), 1)
    eye = jnp.where(ri == ci, 1.0, 0.0)
    x1 = gram * (1.0 / delta) - eye
    x2 = jnp.dot(x1, x1, precision=HIGHEST, preferred_element_type=jnp.float32)
    solver = (
        terms[0] * eye
        + terms[1] * x1
        + terms[2] * x2
        + jnp.dot(
            x2, terms[3] * x1 + terms[4] * x2, precision=HIGHEST, preferred_element_type=jnp.float32
        )
    )

    mine = pl.ds(pl.multiple_of(me * CHUNK, CHUNK), CHUNK)
    for it in range(ITERS):
        projected = jnp.zeros((RESP, CAP), jnp.float32)
        for part in range(8):
            cols = slice(part * 512, (part + 1) * 512)
            projected = projected + lax.dot_general(
                tb[:, cols], design[:, cols], NT, preferred_element_type=jnp.float32
            )
        projected = projected * (1.0 / CAP)
        weights = jnp.dot(
            projected, solver, precision=HIGHEST, preferred_element_type=jnp.float32
        ).astype(jnp.bfloat16)
        if it:
            left(outgoing.at[pl.ds(0, tm - 1)], SCATTER + it - 1)
        for part in range(8):
            cols = slice(part * 512, (part + 1) * 512)
            back = jnp.dot(weights, design[:, cols], preferred_element_type=jnp.float32)
            value = (cross[:, cols] - back) * (1.0 / RHO)
            v[:, cols] = value
            for c in range(4):
                outgoing[part * 4 + c] = value[:, c * CHUNK : (c + 1) * CHUNK].astype(jnp.bfloat16)

        @pl.loop(1, tm)
        def _(i):
            peer = tm_peer(i)
            send(outgoing.at[peer], incoming.at[i - 1], SCATTER + it, {"tm": peer})

        arrived(incoming, SCATTER + it)
        mean = v[:, mine]
        for i in range(tm - 1):
            mean = mean + incoming[i].astype(jnp.float32)
        mean = mean * (1.0 / tm)
        if it:
            mean = mean + z[:, mine]
        if it + 1 < ITERS:
            if it:
                left(gathered.at[pl.ds(0, tm - 1)], GATHER + it - 1)
            gathered[me] = mean.astype(jnp.bfloat16)
            to_tm(gathered.at[me], gathered.at[me], GATHER + it)
            arrived(gathered.at[pl.ds(0, tm - 1)], GATHER + it)
            lengths = []
            for c in range(tm):
                block = gathered[c].astype(jnp.float32)
                lengths.append(jnp.sqrt(jnp.sum(block * block, axis=0, keepdims=True)))
            level = (
                jnp.sum(functools.reduce(jnp.add, lengths), axis=1, keepdims=True)
                * (SHRINK / FEAT)
            )
            for c in range(tm):
                cols = slice(c * CHUNK, (c + 1) * CHUNK)
                factor = jnp.maximum(lengths[c] - level, 0.0) / jnp.maximum(lengths[c], level)
                fresh = gathered[c].astype(jnp.float32) * factor
                dual = v[:, cols] - fresh
                if it:
                    dual = dual + z[:, cols]
                z[:, cols] = fresh
                tb[:, cols] = (cross[:, cols] + RHO * (fresh - dual)).astype(jnp.bfloat16)

    length = jnp.sqrt(jnp.sum(mean * mean, axis=0, keepdims=True))
    norms[me] = length
    to_tm(norms.at[me], norms.at[me], NORMS)
    arrived(norms.at[pl.ds(0, tm - 1)], NORMS)
    level = jnp.sum(jnp.sum(norms[...], axis=0), axis=1, keepdims=True) * (SHRINK / FEAT)
    factor = jnp.maximum(length - level, 0.0) / jnp.maximum(length, level)
    zx[b] = (mean * factor).astype(jnp.bfloat16)
    to_boots(zx.at[b], zx.at[b], BOOTS)
    arrived(sup.at[pl.ds(0, boots - 1)], SUPPORT)
    quarter = pl.ds(pl.multiple_of(lax.rem(me, 4) * CHUNK, CHUNK), CHUNK)
    chosen = sup[me // 4, :, quarter].astype(jnp.float32)
    tally = jnp.maximum(jnp.sum(chosen, axis=0, keepdims=True), 1.0)
    arrived(zx.at[pl.ds(0, boots - 1)], BOOTS)
    average = jnp.zeros((RESP, CHUNK), jnp.float32)
    for k in range(boots):
        average = average + chosen[k : k + 1] * zx[k].astype(jnp.float32)
    average = average / tally
    final[me] = average.astype(jnp.bfloat16)
    to_tm(final.at[me], final.at[me], FINAL)
    normed = jnp.transpose(ext[HEAD : HEAD + SEG, :CHUNK].astype(jnp.float32))[:RESP]
    arrived(final.at[pl.ds(0, tm - 1)], FINAL)
    for c in range(4):
        avg_ref[:, c * CHUNK : (c + 1) * CHUNK] = final[4 * b + c].astype(jnp.float32)
    stacked = jnp.concatenate(
        [
            jnp.concatenate([final[lag * 8 + c] for c in range(8)], axis=1)
            for lag in range(LAGS)
        ],
        axis=0,
    )
    forecast = lax.dot_general(stacked, ext[...], NT, preferred_element_type=jnp.float32)
    residual = normed
    for lag in range(LAGS):
        begin = HEAD - 1 - lag
        turned = pltpu.roll(forecast[lag * RESP : (lag + 1) * RESP], WINDOW - begin, 1)
        residual = residual - turned[:, :SEG]
    res_ref[...] = residual

    left(power.at[pl.ds(0, tm - 1)], POWER)
    left(halo, HALO)
    left(sup.at[pl.ds(0, boots - 1)], SUPPORT)
    left(outgoing.at[pl.ds(0, tm - 1)], SCATTER + ITERS - 1)
    left(gathered.at[pl.ds(0, tm - 1)], GATHER + ITERS - 2)
    left(norms.at[pl.ds(0, tm - 1)], NORMS)
    left(zx.at[pl.ds(0, boots - 1)], BOOTS)
    left(final.at[pl.ds(0, tm - 1)], FINAL)


def per_device(recording, starts, lengths, support):
    tm = lax.axis_size("tm")
    boots = lax.axis_size("boot")
    vmem = pl.BlockSpec(memory_space=pltpu.VMEM)
    smem = pl.BlockSpec(memory_space=pltpu.SMEM)
    return pl.pallas_call(
        functools.partial(kernel, tm, boots),
        out_shape=(
            jax.ShapeDtypeStruct((RESP, FEAT // boots), jnp.float32),
            jax.ShapeDtypeStruct((RESP, SEG), jnp.float32),
        ),
        in_specs=[vmem, smem, smem, vmem],
        out_specs=(vmem, vmem),
        scratch_shapes=[
            pltpu.VMEM((HEAD, CHANNELS), jnp.bfloat16),
            pltpu.VMEM((tm, 1, CHANNELS), jnp.float32),
            pltpu.VMEM((boots, boots, FEAT // boots), jnp.int32),
            pltpu.VMEM((WINDOW, CHANNELS), jnp.bfloat16),
            pltpu.VMEM((CAP, FEAT), jnp.bfloat16),
            pltpu.VMEM((RESP, FEAT), jnp.float32),
            pltpu.VMEM((RESP, FEAT), jnp.float32),
            pltpu.VMEM((RESP, FEAT), jnp.float32),
            pltpu.VMEM((RESP, FEAT), jnp.bfloat16),
            pltpu.VMEM((tm, RESP, CHUNK), jnp.bfloat16),
            pltpu.VMEM((tm - 1, RESP, CHUNK), jnp.bfloat16),
            pltpu.VMEM((tm, RESP, CHUNK), jnp.bfloat16),
            pltpu.VMEM((tm, 1, CHUNK), jnp.float32),
            pltpu.VMEM((boots, RESP, CHUNK), jnp.bfloat16),
            pltpu.VMEM((tm, RESP, CHUNK), jnp.bfloat16),
            pltpu.SemaphoreType.DMA((PHASES,)),
            pltpu.SemaphoreType.DMA((PHASES,)),
        ],
        compiler_params=pltpu.CompilerParams(
            collective_id=0, has_side_effects=True, vmem_limit_bytes=48 * 1024 * 1024
        ),
    )(recording, starts, lengths, support)


def solution(mesh):
    in_specs = (P("tm", None), P("boot", "tm"), P("boot", "tm"), P(None, "boot"))
    out_specs = (P(None, "boot"), P(None, "tm"))
    return jax.shard_map(
        per_device, mesh=mesh, in_specs=in_specs, out_specs=out_specs, check_vma=False
    )
```

time: 610 us -> 90.9 us (0.15)
  waiting for transfers between devices: 460 us -> 0 us
  Pallas kernels: 0 us -> 85.5 us
  blocking collectives: 65.3 us -> 0 us
  matrix products: 23.9 us -> 0 us
  other arithmetic: 20.7 us -> 0 us
  between operations: 17.4 us -> 0.65 us
  local copies, waits for them, and re-layouts: 15.9 us -> 4.51 us
    psum x4 -> x0, waiting for transfers between devices: 405 us -> none  [the longest x3 339 us: per_device(): mean_value = lax.psum(stacked, 'tm') / shards]
    pallas_call x0 -> x1, Pallas kernels: none -> 85.5 us  [per_device(): pl.pallas_call(functools.partial(kernel, tm, boots), out_shape=(jax.Shape...]
    psum x1 -> x0, blocking collectives: 65.3 us -> none  [per_device(): power = lax.psum(jnp.sum(values * values, axis=0), 'tm')]
    all_gather x1 -> x0, waiting for transfers between devices: 54.4 us -> none  [per_device(): everything = lax.all_gather(consensus, 'boot', axis=0, tiled=True)]
    dot_general x21 -> x0, matrix products: 23.9 us -> none  [the longest x3 7.85 us: per_device(): jnp.einsum('brf,bcf->brc', target.astype(jnp.bfloat16), design, preferred...]
    gather x5 -> x0, local copies, waits for them, and re-layouts: 12.2 us -> none  [the longest x4 10.8 us: bootstrap_rows(): jnp.take(window, times + LAGS - 1 - delay_step, axis=0)]
    reduce_sum x11 -> x0, other arithmetic: 6.88 us -> none  [the longest x3 3.37 us: per_device(): norms = jnp.sqrt(jnp.sum(mean_value * mean_value, axis=1))]
  transfers between devices with their start and end apart: 6 -> 0, of which waited for: 6 -> 0; matrix products, arithmetic and copies ran while one was open for 1% -> 0% of each run, Pallas kernels for 0% -> 0%
where the time goes in v1:
time: 90.9 us; the launch traced here: 90.7 us
  Pallas kernels  85.5 us (94%)
  local copies, waits for them, and re-layouts  4.51 us (5%)
    pallas_call x1, Pallas kernels, per_device(): pl.pallas_call(functools.partial(kernel, tm, boots), out_shape=(jax.Shape...  85.5 us
    unnamed x10, local copies, waits for them, and re-layouts  4.51 us

profile of v1, /device:TPU:1, one launch (start us, length us, event | category | flops | bytes accessed | tf_op | source)
XLA Modules:
  0.0 90.7 jit_solution(2264996521258550500)
XLA Ops:
  0.6 0.0 copy-start
  0.6 1.2 %copy-done = bf16[512,1024]{1,0:T(8,128)(2,1)S(1)} copy-done((bf16[512,1024]{1,0:T(8,128)(2,1)S(1)}, bf16[512,1024]{1,0:T(8,128)(2,1)}, u32[]{:S(2)}) %copy-start) | copy-done | bytes 1048600
  1.9 0.0 copy-start.1
  1.9 0.7 copy-done.1
  2.6 0.0 copy-start.2
  2.6 0.7 copy-done.2
  3.2 0.0 copy-start.3
  3.2 0.7 copy-done.3
  3.9 85.5 %shard_map.59 = (f32[32,512]{1,0:T(8,128)S(1)}, f32[32,512]{1,0:T(8,128)S(1)}) custom-call(bf16[512,1024]{1,0:T(8,128)(2,1)S(1)} %copy-done, s32[1,6]{1,0:T(1,128)S(1)} %copy-done.2, s32[1,6]{1,0:T(1,128)S(1)} %copy-done.3, s32[8,512]{1,0:T(8,128)S(1)} %copy-done.1), custom_call_target="tpu_custom_call" | custom-call | tf_op jit(solution)/shard_map/pallas_call | solution.py:330
  89.4 0.6 copy.8
  90.1 0.6 copy.9
Async XLA Ops:
  0.6 1.2 %copy-start = (bf16[512,1024]{1,0:T(8,128)(2,1)S(1)}, bf16[512,1024]{1,0:T(8,128)(2,1)}, u32[]{:S(2)}) copy-start(bf16[512,1024]{1,0:T(8,128)(2,1)} %rec_ref.1) | copy-start | bytes 3145732
  1.9 0.7 copy-start.1
  2.6 0.7 copy-start.2
  3.2 0.7 copy-start.3

commit v2 on v1

--- a/solution.py
+++ b/solution.py
@@ -28,6 +28,27 @@
 NT = (((1,), (1,)), ((), ()))
 HALO, POWER, SUPPORT, SCATTER, GATHER, NORMS, BOOTS, FINAL = 0, 1, 2, 3, 6, 8, 9, 10
 PHASES = 11
+
+
+def chebyshev(gram, rhs, bound):
+    theta = RHO + 0.5 * bound
+    delta = 0.5 * bound
+    sigma = theta / delta
+    total = jnp.zeros_like(rhs)
+    remain = rhs
+    factor = 1.0 / sigma
+    update = rhs / theta
+    for count in range(CHEB):
+        total = total + update
+        if count + 1 < CHEB:
+            applied = RHO * update + jnp.dot(
+                update, gram, precision=HIGHEST, preferred_element_type=jnp.float32
+            )
+            remain = remain - applied
+            after = 1.0 / (2.0 * sigma - factor)
+            update = after * factor * update + 2.0 * after / delta * remain
+            factor = after
+    return total
 
 
 def chebyshev_terms(bound):
@@ -56,15 +77,24 @@
     return total, delta
 
 
+def far_first():
+    offsets = [(d, p, a, c) for d in range(4) for p in range(2) for a in range(2) for c in range(2)]
+    hops = {o: min(o[0], 4 - o[0]) + (2 if o[1] > o[2] else o[1] | o[2]) for o in offsets}
+    return sorted(offsets[1:], key=lambda o: -hops[o])
+
+
 def kernel(
     tm,
     boots,
-    rec_ref,
+    rec_hbm,
+    starts_hbm,
+    lengths_hbm,
+    support_hbm,
+    avg_ref,
+    res_ref,
+    rec,
     starts_ref,
     lengths_ref,
-    support_ref,
-    avg_ref,
-    res_ref,
     halo,
     power,
     sup,
@@ -74,6 +104,8 @@
     v,
     z,
     tb,
+    solver,
+    flat,
     outgoing,
     incoming,
     gathered,
@@ -82,9 +114,16 @@
     final,
     send_sem,
     recv_sem,
+    local_sem,
 ):
     b = lax.axis_index("boot")
     me = lax.axis_index("tm")
+    x, y, core = me // 8, lax.rem(me // 2, 4), lax.rem(me, 2)
+    offsets = far_first()
+
+    def tm_at(o):
+        pair, place = lax.rem(y // 2 + o[1], 2), lax.rem(lax.rem(y, 2) + o[2], 2)
+        return lax.rem(x + o[0], 4) * 8 + pair * 4 + place * 2 + lax.rem(core + o[3], 2)
 
     def tm_peer(i):
         return lax.rem(me + i, tm)
@@ -105,6 +144,16 @@
         pl.semaphore_signal(
             barrier, inc=1, device_id={"boot": boot_peer(i)}, device_id_type=pl.DeviceIdType.MESH
         )
+
+    def fetch(src, dst, k):
+        copy = pltpu.make_async_copy(src, dst, local_sem.at[k])
+        copy.start()
+        return copy
+
+    rec_copy = fetch(rec_hbm, rec, 0)
+    starts_copy = fetch(starts_hbm, starts_ref, 1)
+    lengths_copy = fetch(lengths_hbm, lengths_ref, 2)
+    support_copy = fetch(support_hbm, sup.at[b], 3)
 
     def send(src, dst, phase, target):
         pltpu.make_async_remote_copy(
@@ -117,13 +166,11 @@
         ).start()
 
     def to_tm(src, dst, phase):
-        @pl.loop(1, tm)
-        def _(i):
-            send(src, dst, phase, {"tm": tm_peer(i)})
+        for o in offsets:
+            send(src, dst, phase, {"tm": tm_at(o)})
 
     def to_boots(src, dst, phase):
-        @pl.loop(1, boots)
-        def _(i):
+        for i in (4, 3, 5, 2, 6, 1, 7):
             send(src, dst, phase, {"boot": boot_peer(i)})
 
     def arrived(ref, phase):
@@ -132,89 +179,83 @@
     def left(ref, phase):
         pltpu.make_async_copy(ref, ref, send_sem.at[phase]).wait()
 
+    rec_copy.wait()
     acc = jnp.zeros((8, CHANNELS), jnp.float32)
 
     def add_rows(k, acc):
-        block = rec_ref[pl.ds(pl.multiple_of(k * 16, 16), 16), :].astype(jnp.float32)
+        block = rec[pl.ds(pl.multiple_of(k * 16, 16), 16), :].astype(jnp.float32)
         block = block * block
         return acc + block[:8] + block[8:]
 
     acc = lax.fori_loop(0, SEG // 16, add_rows, acc)
     power[me] = jnp.sum(acc, axis=0, keepdims=True)
 
-    pl.semaphore_wait(barrier, tm + boots - 2)
-    to_tm(power.at[me], power.at[me], POWER)
-    send(rec_ref.at[pl.ds(SEG - HEAD, HEAD)], halo, HALO, {"tm": tm_peer(1)})
-    to_boots(support_ref, sup.at[b], SUPPORT)
-    sup[b] = support_ref[...]
-
+    starts_copy.wait()
+    lengths_copy.wait()
     row = lax.broadcasted_iota(jnp.int32, (CAP, CHUNK), 0)
-    place = jnp.full((CAP, CHUNK), -4 * WINDOW, jnp.int32)
+    place = jnp.full((CAP, CHUNK), -4 * SEG, jnp.int32)
     offset = jnp.int32(0)
     for k in range(NBLK):
         length = lengths_ref[0, k]
         inside = (row >= offset) & (row < offset + length)
-        place = jnp.where(inside, row + (starts_ref[0, k] - offset + HEAD), place)
+        place = jnp.where(inside, row + (starts_ref[0, k] - offset), place)
         offset = offset + length
     lane = lax.broadcasted_iota(jnp.int32, (CAP, CHUNK), 1)
 
-    def picks(back):
+    def picks(back, width):
         return jnp.concatenate(
             [
                 jnp.where(place - back == lane + c * CHUNK, 1.0, 0.0).astype(jnp.bfloat16)
-                for c in range(WINDOW // CHUNK)
+                for c in range(width // CHUNK)
             ],
             axis=1,
         )
 
+    def raw_rows(lag):
+        pick = picks(1 + lag, SEG)
+        for part in range(4):
+            at = lag * CHANNELS + part * 256
+            design[:, at : at + 256] = jnp.dot(
+                pick, rec[:, part * 256 : (part + 1) * 256], preferred_element_type=jnp.float32
+            ).astype(jnp.bfloat16)
+
+    support_copy.wait()
+    raw_rows(0)
+    pl.semaphore_wait(barrier, tm + boots - 2)
+    send(rec_hbm.at[pl.ds(SEG - HEAD, HEAD)], halo, HALO, {"tm": tm_peer(1)})
+    to_tm(power.at[me], power.at[me], POWER)
+    to_boots(support_hbm, sup.at[b], SUPPORT)
+    raw_rows(1)
+    raw_rows(2)
+    raw_rows(3)
+    answer = jnp.dot(picks(0, SEG), rec[:, :CHUNK], preferred_element_type=jnp.float32)
+    arrived(halo, HALO)
+    before = halo[...]
+    before = jnp.where(me == 0, jnp.zeros_like(before), before)
+    behind = lane - HEAD
+    for lag in range(LAGS):
+        cols = slice(lag * CHANNELS, (lag + 1) * CHANNELS)
+        reach = jnp.where(place - 1 - lag == behind, 1.0, 0.0).astype(jnp.bfloat16)[:, :HEAD]
+        extra = jnp.dot(reach, before, preferred_element_type=jnp.float32)
+        design[:, cols] = (design[:, cols].astype(jnp.float32) + extra).astype(jnp.bfloat16)
     arrived(power.at[pl.ds(0, tm - 1)], POWER)
     total = jnp.sum(power[...], axis=0)
     scale = 1.0 / jnp.sqrt(total / (SEG * tm) + EPSILON)
 
-    def scale_rows(k, carry):
-        at = pl.multiple_of(k * 16, 16)
-        block = rec_ref[pl.ds(at, 16), :].astype(jnp.float32) * scale
-        ext[pl.ds(pl.multiple_of(at + HEAD, 16), 16), :] = block.astype(jnp.bfloat16)
-        return carry
-
-    lax.fori_loop(0, SEG // 16, scale_rows, 0)
-    arrived(halo, HALO)
-    first = (halo[...].astype(jnp.float32) * scale).astype(jnp.bfloat16)
-    ext[0:HEAD, :] = jnp.where(me == 0, jnp.zeros_like(first), first)
-    ext[HEAD + SEG :, :] = jnp.zeros((WINDOW - HEAD - SEG, CHANNELS), jnp.bfloat16)
-
-    answer = jnp.dot(picks(0), ext[:, :CHUNK], preferred_element_type=jnp.float32)
+    answer = (answer * scale[:, :CHUNK]).astype(jnp.bfloat16).astype(jnp.float32)
     answer = jnp.transpose(answer)[:RESP].astype(jnp.bfloat16)
     gram = jnp.zeros((CAP, CAP), jnp.float32)
     for lag in range(LAGS):
-        pick = picks(1 + lag)
-        for part in range(4):
-            at = lag * CHANNELS + part * 256
-            block = jnp.dot(
-                pick, ext[:, part * 256 : (part + 1) * 256], preferred_element_type=jnp.float32
-            ).astype(jnp.bfloat16)
-            design[:, at : at + 256] = block
-            fit = jnp.dot(answer, block, preferred_element_type=jnp.float32) * (1.0 / CAP)
-            cross[:, at : at + 256] = fit
-            tb[:, at : at + 256] = fit.astype(jnp.bfloat16)
-        piece = design[:, lag * CHANNELS : (lag + 1) * CHANNELS]
+        cols = slice(lag * CHANNELS, (lag + 1) * CHANNELS)
+        piece = (design[:, cols].astype(jnp.float32) * scale).astype(jnp.bfloat16)
+        design[:, cols] = piece
         gram = gram + lax.dot_general(piece, piece, NT, preferred_element_type=jnp.float32)
+        fit = jnp.dot(answer, piece, preferred_element_type=jnp.float32) * (1.0 / CAP)
+        cross[:, cols] = fit
+        tb[:, cols] = fit.astype(jnp.bfloat16)
     gram = gram * (1.0 / CAP)
+    solver[...] = gram
     bound = jnp.sqrt(jnp.sum(jnp.sum(gram * gram, axis=1, keepdims=True), axis=0, keepdims=True))
-    terms, delta = chebyshev_terms(bound)
-    ri = lax.broadcasted_iota(jnp.int32, (CAP, CAP), 0)
-    ci = lax.broadcasted_iota(jnp.int32, (CAP, CAP), 1)
-    eye = jnp.where(ri == ci, 1.0, 0.0)
-    x1 = gram * (1.0 / delta) - eye
-    x2 = jnp.dot(x1, x1, precision=HIGHEST, preferred_element_type=jnp.float32)
-    solver = (
-        terms[0] * eye
-        + terms[1] * x1
-        + terms[2] * x2
-        + jnp.dot(
-            x2, terms[3] * x1 + terms[4] * x2, precision=HIGHEST, preferred_element_type=jnp.float32
-        )
-    )
 
     mine = pl.ds(pl.multiple_of(me * CHUNK, CHUNK), CHUNK)
     for it in range(ITERS):
@@ -225,23 +266,60 @@
                 tb[:, cols], design[:, cols], NT, preferred_element_type=jnp.float32
             )
         projected = projected * (1.0 / CAP)
-        weights = jnp.dot(
-            projected, solver, precision=HIGHEST, preferred_element_type=jnp.float32
-        ).astype(jnp.bfloat16)
+        if it == 0:
+            flat[...] = projected
+            weights = chebyshev(solver[...], projected, bound)
+            flat[...] = weights
+        else:
+            weights = jnp.dot(
+                projected, solver[...], precision=HIGHEST, preferred_element_type=jnp.float32
+            )
+        weights = weights.astype(jnp.bfloat16)
         if it:
             left(outgoing.at[pl.ds(0, tm - 1)], SCATTER + it - 1)
-        for part in range(8):
-            cols = slice(part * 512, (part + 1) * 512)
+        for dx, dp in ((2, 1), (2, 0), (1, 1), (3, 1), (1, 0), (3, 0), (0, 1), (0, 0)):
+            group = lax.rem(x + dx, 4) * 2 + lax.rem(y // 2 + dp, 2)
+            cols = pl.ds(pl.multiple_of(group * 512, 512), 512)
             back = jnp.dot(weights, design[:, cols], preferred_element_type=jnp.float32)
             value = (cross[:, cols] - back) * (1.0 / RHO)
             v[:, cols] = value
             for c in range(4):
-                outgoing[part * 4 + c] = value[:, c * CHUNK : (c + 1) * CHUNK].astype(jnp.bfloat16)
-
-        @pl.loop(1, tm)
-        def _(i):
-            peer = tm_peer(i)
-            send(outgoing.at[peer], incoming.at[i - 1], SCATTER + it, {"tm": peer})
+                outgoing[group * 4 + c] = value[:, c * CHUNK : (c + 1) * CHUNK].astype(jnp.bfloat16)
+            for slot, o in enumerate(offsets):
+                if o[:2] == (dx, dp):
+                    peer = tm_at(o)
+                    send(outgoing.at[peer], incoming.at[slot], SCATTER + it, {"tm": peer})
+
+        if it == 0:
+            terms, delta = chebyshev_terms(bound)
+            ri = lax.broadcasted_iota(jnp.int32, (CAP, CAP), 0)
+            ci = lax.broadcasted_iota(jnp.int32, (CAP, CAP), 1)
+            eye = jnp.where(ri == ci, 1.0, 0.0)
+            x1 = solver[...] * (1.0 / delta) - eye
+            x2 = jnp.dot(x1, x1, precision=HIGHEST, preferred_element_type=jnp.float32)
+            solver[...] = (
+                terms[0] * eye
+                + terms[1] * x1
+                + terms[2] * x2
+                + jnp.dot(
+                    x2,
+                    terms[3] * x1 + terms[4] * x2,
+                    precision=HIGHEST,
+                    preferred_element_type=jnp.float32,
+                )
+            )
+
+            def scale_rows(k, carry):
+                at = pl.multiple_of(k * 16, 16)
+                block = rec[pl.ds(at, 16), :].astype(jnp.float32) * scale
+                ext[pl.ds(pl.multiple_of(at + HEAD, 16), 16), :] = block.astype(jnp.bfloat16)
+                return carry
+
+            lax.fori_loop(0, SEG // 16, scale_rows, 0)
+            ext[0:HEAD, :] = (before.astype(jnp.float32) * scale).astype(jnp.bfloat16)
+            ext[HEAD + SEG :, :] = jnp.zeros((WINDOW - HEAD - SEG, CHANNELS), jnp.bfloat16)
+            normed = ext[HEAD : HEAD + SEG, :CHUNK].astype(jnp.float32)
+            res_ref[...] = jnp.transpose(normed)[:RESP]
 
         arrived(incoming, SCATTER + it)
         mean = v[:, mine]
@@ -293,7 +371,6 @@
     average = average / tally
     final[me] = average.astype(jnp.bfloat16)
     to_tm(final.at[me], final.at[me], FINAL)
-    normed = jnp.transpose(ext[HEAD : HEAD + SEG, :CHUNK].astype(jnp.float32))[:RESP]
     arrived(final.at[pl.ds(0, tm - 1)], FINAL)
     for c in range(4):
         avg_ref[:, c * CHUNK : (c + 1) * CHUNK] = final[4 * b + c].astype(jnp.float32)
@@ -305,7 +382,7 @@
         axis=0,
     )
     forecast = lax.dot_general(stacked, ext[...], NT, preferred_element_type=jnp.float32)
-    residual = normed
+    residual = res_ref[...]
     for lag in range(LAGS):
         begin = HEAD - 1 - lag
         turned = pltpu.roll(forecast[lag * RESP : (lag + 1) * RESP], WINDOW - begin, 1)
@@ -326,16 +403,19 @@
     tm = lax.axis_size("tm")
     boots = lax.axis_size("boot")
     vmem = pl.BlockSpec(memory_space=pltpu.VMEM)
-    smem = pl.BlockSpec(memory_space=pltpu.SMEM)
+    anywhere = pl.BlockSpec(memory_space=pl.ANY)
     return pl.pallas_call(
         functools.partial(kernel, tm, boots),
         out_shape=(
             jax.ShapeDtypeStruct((RESP, FEAT // boots), jnp.float32),
             jax.ShapeDtypeStruct((RESP, SEG), jnp.float32),
         ),
-        in_specs=[vmem, smem, smem, vmem],
+        in_specs=[anywhere] * 4,
         out_specs=(vmem, vmem),
         scratch_shapes=[
+            pltpu.VMEM((SEG, CHANNELS), jnp.bfloat16),
+            pltpu.SMEM((1, NBLK), jnp.int32),
+            pltpu.SMEM((1, NBLK), jnp.int32),
             pltpu.VMEM((HEAD, CHANNELS), jnp.bfloat16),
             pltpu.VMEM((tm, 1, CHANNELS), jnp.float32),
             pltpu.VMEM((boots, boots, FEAT // boots), jnp.int32),
@@ -345,6 +425,8 @@
             pltpu.VMEM((RESP, FEAT), jnp.float32),
             pltpu.VMEM((RESP, FEAT), jnp.float32),
             pltpu.VMEM((RESP, FEAT), jnp.bfloat16),
+            pltpu.VMEM((CAP, CAP), jnp.float32),
+            pltpu.VMEM((RESP, CAP), jnp.float32),
             pltpu.VMEM((tm, RESP, CHUNK), jnp.bfloat16),
             pltpu.VMEM((tm - 1, RESP, CHUNK), jnp.bfloat16),
             pltpu.VMEM((tm, RESP, CHUNK), jnp.bfloat16),
@@ -353,6 +435,7 @@
             pltpu.VMEM((tm, RESP, CHUNK), jnp.bfloat16),
             pltpu.SemaphoreType.DMA((PHASES,)),
             pltpu.SemaphoreType.DMA((PHASES,)),
+            pltpu.SemaphoreType.DMA((4,)),
         ],
         compiler_params=pltpu.CompilerParams(
             collective_id=0, has_side_effects=True, vmem_limit_bytes=48 * 1024 * 1024

time: 90.9 us -> 76.5 us (0.84)
  Pallas kernels: 85.5 us -> 71.2 us
    pallas_call x1, Pallas kernels: 85.5 us -> 71.2 us  [per_device(): pl.pallas_call(functools.partial(kernel, tm, boots), out_shape=(jax.Shape...]
where the time goes in v2:
time: 76.5 us; the launch traced here: 76.4 us
  Pallas kernels  71.2 us (93%)
  local copies, waits for them, and re-layouts  4.51 us (6%)
    pallas_call x1, Pallas kernels, per_device(): pl.pallas_call(functools.partial(kernel, tm, boots), out_shape=(jax.Shape...  71.2 us
    unnamed x10, local copies, waits for them, and re-layouts  4.51 us

profile of v2, /device:TPU:1, one launch (start us, length us, event | category | flops | bytes accessed | tf_op | source)
XLA Modules:
  0.0 76.4 jit_solution(9743162586599847250)
XLA Ops:
  0.6 0.0 copy-start
  0.6 1.2 %copy-done = bf16[512,1024]{1,0:T(8,128)(2,1)S(1)} copy-done((bf16[512,1024]{1,0:T(8,128)(2,1)S(1)}, bf16[512,1024]{1,0:T(8,128)(2,1)}, u32[]{:S(2)}) %copy-start) | copy-done | bytes 1048600
  1.9 0.0 copy-start.1
  1.9 0.7 copy-done.1
  2.6 0.0 copy-start.2
  2.6 0.7 copy-done.2
  3.2 0.0 copy-start.3
  3.2 0.7 copy-done.3
  3.9 71.2 %shard_map.59 = (f32[32,512]{1,0:T(8,128)S(1)}, f32[32,512]{1,0:T(8,128)S(1)}) custom-call(bf16[512,1024]{1,0:T(8,128)(2,1)S(1)} %copy-done, s32[1,6]{1,0:T(1,128)S(1)} %copy-done.2, s32[1,6]{1,0:T(1,128)S(1)} %copy-done.3, s32[8,512]{1,0:T(8,128)S(1)} %copy-done.1), custom_call_target="tpu_custom_call" | custom-call | tf_op jit(solution)/shard_map/pallas_call | solution.py:407
  75.1 0.6 copy.8
  75.7 0.6 copy.9
Async XLA Ops:
  0.6 1.2 %copy-start = (bf16[512,1024]{1,0:T(8,128)(2,1)S(1)}, bf16[512,1024]{1,0:T(8,128)(2,1)}, u32[]{:S(2)}) copy-start(bf16[512,1024]{1,0:T(8,128)(2,1)} %rec_hbm.1) | copy-start | bytes 3145732
  1.9 0.7 copy-start.1
  2.6 0.7 copy-start.2
  3.2 0.7 copy-start.3

commit v3 on v2

--- a/solution.py
+++ b/solution.py
@@ -90,8 +90,7 @@
     starts_hbm,
     lengths_hbm,
     support_hbm,
-    avg_ref,
-    res_ref,
+    packed,
     rec,
     starts_ref,
     lengths_ref,
@@ -105,7 +104,6 @@
     z,
     tb,
     solver,
-    flat,
     outgoing,
     incoming,
     gathered,
@@ -267,9 +265,7 @@
             )
         projected = projected * (1.0 / CAP)
         if it == 0:
-            flat[...] = projected
             weights = chebyshev(solver[...], projected, bound)
-            flat[...] = weights
         else:
             weights = jnp.dot(
                 projected, solver[...], precision=HIGHEST, preferred_element_type=jnp.float32
@@ -319,7 +315,7 @@
             ext[0:HEAD, :] = (before.astype(jnp.float32) * scale).astype(jnp.bfloat16)
             ext[HEAD + SEG :, :] = jnp.zeros((WINDOW - HEAD - SEG, CHANNELS), jnp.bfloat16)
             normed = ext[HEAD : HEAD + SEG, :CHUNK].astype(jnp.float32)
-            res_ref[...] = jnp.transpose(normed)[:RESP]
+            packed[:RESP] = jnp.transpose(normed)[:RESP]
 
         arrived(incoming, SCATTER + it)
         mean = v[:, mine]
@@ -373,7 +369,7 @@
     to_tm(final.at[me], final.at[me], FINAL)
     arrived(final.at[pl.ds(0, tm - 1)], FINAL)
     for c in range(4):
-        avg_ref[:, c * CHUNK : (c + 1) * CHUNK] = final[4 * b + c].astype(jnp.float32)
+        packed[2 * RESP :, c * CHUNK : (c + 1) * CHUNK] = final[4 * b + c].astype(jnp.float32)
     stacked = jnp.concatenate(
         [
             jnp.concatenate([final[lag * 8 + c] for c in range(8)], axis=1)
@@ -382,12 +378,12 @@
         axis=0,
     )
     forecast = lax.dot_general(stacked, ext[...], NT, preferred_element_type=jnp.float32)
-    residual = res_ref[...]
+    told = jnp.zeros((RESP, SEG), jnp.float32)
     for lag in range(LAGS):
         begin = HEAD - 1 - lag
         turned = pltpu.roll(forecast[lag * RESP : (lag + 1) * RESP], WINDOW - begin, 1)
-        residual = residual - turned[:, :SEG]
-    res_ref[...] = residual
+        told = told + turned[:, :SEG]
+    packed[RESP : 2 * RESP] = told
 
     left(power.at[pl.ds(0, tm - 1)], POWER)
     left(halo, HALO)
@@ -403,15 +399,12 @@
     tm = lax.axis_size("tm")
     boots = lax.axis_size("boot")
     vmem = pl.BlockSpec(memory_space=pltpu.VMEM)
-    anywhere = pl.BlockSpec(memory_space=pl.ANY)
-    return pl.pallas_call(
+    anywhere = pl.BlockSpec(memory_space=pltpu.HBM)
+    packed = pl.pallas_call(
         functools.partial(kernel, tm, boots),
-        out_shape=(
-            jax.ShapeDtypeStruct((RESP, FEAT // boots), jnp.float32),
-            jax.ShapeDtypeStruct((RESP, SEG), jnp.float32),
-        ),
+        out_shape=jax.ShapeDtypeStruct((3 * RESP, SEG), jnp.float32),
         in_specs=[anywhere] * 4,
-        out_specs=(vmem, vmem),
+        out_specs=vmem,
         scratch_shapes=[
             pltpu.VMEM((SEG, CHANNELS), jnp.bfloat16),
             pltpu.SMEM((1, NBLK), jnp.int32),
@@ -426,7 +419,6 @@
             pltpu.VMEM((RESP, FEAT), jnp.float32),
             pltpu.VMEM((RESP, FEAT), jnp.bfloat16),
             pltpu.VMEM((CAP, CAP), jnp.float32),
-            pltpu.VMEM((RESP, CAP), jnp.float32),
             pltpu.VMEM((tm, RESP, CHUNK), jnp.bfloat16),
             pltpu.VMEM((tm - 1, RESP, CHUNK), jnp.bfloat16),
             pltpu.VMEM((tm, RESP, CHUNK), jnp.bfloat16),
@@ -440,7 +432,8 @@
         compiler_params=pltpu.CompilerParams(
             collective_id=0, has_side_effects=True, vmem_limit_bytes=48 * 1024 * 1024
         ),
-    )(recording, starts, lengths, support)
+    )(*(pltpu.with_memory_space_constraint(a, pltpu.HBM) for a in (recording, starts, lengths, support)))
+    return packed[2 * RESP :], packed[:RESP] - packed[RESP : 2 * RESP]
 
 
 def solution(mesh):

time: 76.5 us -> 73.1 us (0.956)
  local copies, waits for them, and re-layouts: 4.51 us -> 0 us
    unnamed x10 -> x0, local copies, waits for them, and re-layouts: 4.51 us -> none
where the time goes in v3:
time: 73.1 us; the launch traced here: 72.9 us
  Pallas kernels  71.6 us (98%)
    pallas_call x1, Pallas kernels, per_device(): pl.pallas_call(functools.partial(kernel, tm, boots), out_shape=jax.ShapeD...  71.6 us

profile of v3, /device:TPU:1, one launch (start us, length us, event | category | flops | bytes accessed | tf_op | source)
XLA Modules:
  0.0 72.9 jit_solution(9115859778257255356)
XLA Ops:
  0.6 71.6 %shard_map.59 = f32[96,512]{1,0:T(8,128)S(1)} custom-call(bf16[512,1024]{1,0:T(8,128)(2,1)} %rec_hbm.1, s32[1,6]{1,0:T(1,128)} %starts_hbm.1, s32[1,6]{1,0:T(1,128)} %lengths_hbm.1, s32[8,512]{1,0:T(8,128)} %support_hbm.1), custom_call_target="tpu_custom_call" | custom-call | tf_op jit(solution)/shard_map/pallas_call | solution.py:403
  72.3 0.7 slice_subtract_fusion

commit v4 on v3

--- a/solution.py
+++ b/solution.py
@@ -26,11 +26,27 @@
 
 HIGHEST = lax.Precision.HIGHEST
 NT = (((1,), (1,)), ((), ()))
+NN = (((1,), (0,)), ((), ()))
 HALO, POWER, SUPPORT, SCATTER, GATHER, NORMS, BOOTS, FINAL = 0, 1, 2, 3, 6, 8, 9, 10
 PHASES = 11
 
 
+def split(a):
+    high = a.astype(jnp.bfloat16)
+    return high, (a - high.astype(jnp.float32)).astype(jnp.bfloat16)
+
+
+def times(a, high, low):
+    rows = a.shape[0]
+    first, rest = split(a)
+    out = jnp.dot(
+        jnp.concatenate([first, rest], axis=0), high, preferred_element_type=jnp.float32
+    )
+    return out[:rows] + (out[rows:] + jnp.dot(first, low, preferred_element_type=jnp.float32))
+
+
 def chebyshev(gram, rhs, bound):
+    high, low = split(gram)
     theta = RHO + 0.5 * bound
     delta = 0.5 * bound
     sigma = theta / delta
@@ -41,9 +57,7 @@
     for count in range(CHEB):
         total = total + update
         if count + 1 < CHEB:
-            applied = RHO * update + jnp.dot(
-                update, gram, precision=HIGHEST, preferred_element_type=jnp.float32
-            )
+            applied = RHO * update + times(update, high, low)
             remain = remain - applied
             after = 1.0 / (2.0 * sigma - factor)
             update = after * factor * update + 2.0 * after / delta * remain
@@ -99,11 +113,13 @@
     sup,
     ext,
     design,
+    turned,
     cross,
     v,
     z,
-    tb,
     solver,
+    solver_high,
+    solver_low,
     outgoing,
     incoming,
     gathered,
@@ -243,6 +259,7 @@
     answer = (answer * scale[:, :CHUNK]).astype(jnp.bfloat16).astype(jnp.float32)
     answer = jnp.transpose(answer)[:RESP].astype(jnp.bfloat16)
     gram = jnp.zeros((CAP, CAP), jnp.float32)
+    projected = jnp.zeros((RESP, CAP), jnp.float32)
     for lag in range(LAGS):
         cols = slice(lag * CHANNELS, (lag + 1) * CHANNELS)
         piece = (design[:, cols].astype(jnp.float32) * scale).astype(jnp.bfloat16)
@@ -250,26 +267,24 @@
         gram = gram + lax.dot_general(piece, piece, NT, preferred_element_type=jnp.float32)
         fit = jnp.dot(answer, piece, preferred_element_type=jnp.float32) * (1.0 / CAP)
         cross[:, cols] = fit
-        tb[:, cols] = fit.astype(jnp.bfloat16)
+        projected = projected + lax.dot_general(
+            fit.astype(jnp.bfloat16), piece, NT, preferred_element_type=jnp.float32
+        )
     gram = gram * (1.0 / CAP)
     solver[...] = gram
     bound = jnp.sqrt(jnp.sum(jnp.sum(gram * gram, axis=1, keepdims=True), axis=0, keepdims=True))
 
+    def flip(lag):
+        cols = slice(lag * CHANNELS, (lag + 1) * CHANNELS)
+        turned[cols, :] = jnp.transpose(design[:, cols])
+
     mine = pl.ds(pl.multiple_of(me * CHUNK, CHUNK), CHUNK)
     for it in range(ITERS):
-        projected = jnp.zeros((RESP, CAP), jnp.float32)
-        for part in range(8):
-            cols = slice(part * 512, (part + 1) * 512)
-            projected = projected + lax.dot_general(
-                tb[:, cols], design[:, cols], NT, preferred_element_type=jnp.float32
-            )
         projected = projected * (1.0 / CAP)
         if it == 0:
             weights = chebyshev(solver[...], projected, bound)
         else:
-            weights = jnp.dot(
-                projected, solver[...], precision=HIGHEST, preferred_element_type=jnp.float32
-            )
+            weights = times(projected, solver_high[...], solver_low[...])
         weights = weights.astype(jnp.bfloat16)
         if it:
             left(outgoing.at[pl.ds(0, tm - 1)], SCATTER + it - 1)
@@ -293,7 +308,7 @@
             eye = jnp.where(ri == ci, 1.0, 0.0)
             x1 = solver[...] * (1.0 / delta) - eye
             x2 = jnp.dot(x1, x1, precision=HIGHEST, preferred_element_type=jnp.float32)
-            solver[...] = (
+            solver_high[...], solver_low[...] = split(
                 terms[0] * eye
                 + terms[1] * x1
                 + terms[2] * x2
@@ -305,17 +320,7 @@
                 )
             )
 
-            def scale_rows(k, carry):
-                at = pl.multiple_of(k * 16, 16)
-                block = rec[pl.ds(at, 16), :].astype(jnp.float32) * scale
-                ext[pl.ds(pl.multiple_of(at + HEAD, 16), 16), :] = block.astype(jnp.bfloat16)
-                return carry
-
-            lax.fori_loop(0, SEG // 16, scale_rows, 0)
-            ext[0:HEAD, :] = (before.astype(jnp.float32) * scale).astype(jnp.bfloat16)
-            ext[HEAD + SEG :, :] = jnp.zeros((WINDOW - HEAD - SEG, CHANNELS), jnp.bfloat16)
-            normed = ext[HEAD : HEAD + SEG, :CHUNK].astype(jnp.float32)
-            packed[:RESP] = jnp.transpose(normed)[:RESP]
+            flip(0)
 
         arrived(incoming, SCATTER + it)
         mean = v[:, mine]
@@ -329,6 +334,22 @@
                 left(gathered.at[pl.ds(0, tm - 1)], GATHER + it - 1)
             gathered[me] = mean.astype(jnp.bfloat16)
             to_tm(gathered.at[me], gathered.at[me], GATHER + it)
+            if it == 0:
+                flip(1)
+                flip(2)
+                flip(3)
+            else:
+                def scale_rows(k, carry):
+                    at = pl.multiple_of(k * 16, 16)
+                    block = rec[pl.ds(at, 16), :].astype(jnp.float32) * scale
+                    ext[pl.ds(pl.multiple_of(at + HEAD, 16), 16), :] = block.astype(jnp.bfloat16)
+                    return carry
+
+                lax.fori_loop(0, SEG // 16, scale_rows, 0)
+                ext[0:HEAD, :] = (before.astype(jnp.float32) * scale).astype(jnp.bfloat16)
+                ext[HEAD + SEG :, :] = jnp.zeros((WINDOW - HEAD - SEG, CHANNELS), jnp.bfloat16)
+                normed = ext[HEAD : HEAD + SEG, :CHUNK].astype(jnp.float32)
+                packed[:RESP] = jnp.transpose(normed)[:RESP]
             arrived(gathered.at[pl.ds(0, tm - 1)], GATHER + it)
             lengths = []
             for c in range(tm):
@@ -338,16 +359,24 @@
                 jnp.sum(functools.reduce(jnp.add, lengths), axis=1, keepdims=True)
                 * (SHRINK / FEAT)
             )
-            for c in range(tm):
-                cols = slice(c * CHUNK, (c + 1) * CHUNK)
-                factor = jnp.maximum(lengths[c] - level, 0.0) / jnp.maximum(lengths[c], level)
-                fresh = gathered[c].astype(jnp.float32) * factor
-                dual = v[:, cols] - fresh
-                if it:
-                    dual = dual + z[:, cols]
-                z[:, cols] = fresh
-                tb[:, cols] = (cross[:, cols] + RHO * (fresh - dual)).astype(jnp.bfloat16)
-
+            projected = jnp.zeros((RESP, CAP), jnp.float32)
+            for part in range(8):
+                targets = []
+                for c in range(part * 4, part * 4 + 4):
+                    cols = slice(c * CHUNK, (c + 1) * CHUNK)
+                    factor = jnp.maximum(lengths[c] - level, 0.0) / jnp.maximum(lengths[c], level)
+                    fresh = gathered[c].astype(jnp.float32) * factor
+                    dual = v[:, cols] - fresh
+                    if it:
+                        dual = dual + z[:, cols]
+                    z[:, cols] = fresh
+                    targets.append((cross[:, cols] + RHO * (fresh - dual)).astype(jnp.bfloat16))
+                projected = projected + lax.dot_general(
+                    jnp.concatenate(targets, axis=1),
+                    turned[part * 512 : (part + 1) * 512, :],
+                    NN,
+                    preferred_element_type=jnp.float32,
+                )
     length = jnp.sqrt(jnp.sum(mean * mean, axis=0, keepdims=True))
     norms[me] = length
     to_tm(norms.at[me], norms.at[me], NORMS)
@@ -381,8 +410,8 @@
     told = jnp.zeros((RESP, SEG), jnp.float32)
     for lag in range(LAGS):
         begin = HEAD - 1 - lag
-        turned = pltpu.roll(forecast[lag * RESP : (lag + 1) * RESP], WINDOW - begin, 1)
-        told = told + turned[:, :SEG]
+        shifted = pltpu.roll(forecast[lag * RESP : (lag + 1) * RESP], WINDOW - begin, 1)
+        told = told + shifted[:, :SEG]
     packed[RESP : 2 * RESP] = told
 
     left(power.at[pl.ds(0, tm - 1)], POWER)
@@ -414,11 +443,13 @@
             pltpu.VMEM((boots, boots, FEAT // boots), jnp.int32),
             pltpu.VMEM((WINDOW, CHANNELS), jnp.bfloat16),
             pltpu.VMEM((CAP, FEAT), jnp.bfloat16),
+            pltpu.VMEM((FEAT, CAP), jnp.bfloat16),
             pltpu.VMEM((RESP, FEAT), jnp.float32),
             pltpu.VMEM((RESP, FEAT), jnp.float32),
             pltpu.VMEM((RESP, FEAT), jnp.float32),
-            pltpu.VMEM((RESP, FEAT), jnp.bfloat16),
             pltpu.VMEM((CAP, CAP), jnp.float32),
+            pltpu.VMEM((CAP, CAP), jnp.bfloat16),
+            pltpu.VMEM((CAP, CAP), jnp.bfloat16),
             pltpu.VMEM((tm, RESP, CHUNK), jnp.bfloat16),
             pltpu.VMEM((tm - 1, RESP, CHUNK), jnp.bfloat16),
             pltpu.VMEM((tm, RESP, CHUNK), jnp.bfloat16),

time: 73.1 us -> 70.4 us (0.963)
  Pallas kernels: 71.6 us -> 69 us
    pallas_call x1, Pallas kernels: 71.6 us -> 69 us  [per_device(): pl.pallas_call(functools.partial(kernel, tm, boots), out_shape=jax.ShapeD...]
where the time goes in v4:
time: 70.4 us; the launch traced here: 70.3 us
  Pallas kernels  69 us (98%)
    pallas_call x1, Pallas kernels, per_device(): pl.pallas_call(functools.partial(kernel, tm, boots), out_shape=jax.ShapeD...  69 us

profile of v4, /device:TPU:1, one launch (start us, length us, event | category | flops | bytes accessed | tf_op | source)
XLA Modules:
  0.0 70.3 jit_solution(7110255374545511691)
XLA Ops:
  0.6 69.0 %shard_map.59 = f32[96,512]{1,0:T(8,128)S(1)} custom-call(bf16[512,1024]{1,0:T(8,128)(2,1)} %rec_hbm.1, s32[1,6]{1,0:T(1,128)} %starts_hbm.1, s32[1,6]{1,0:T(1,128)} %lengths_hbm.1, s32[8,512]{1,0:T(8,128)} %support_hbm.1), custom_call_target="tpu_custom_call" | custom-call | tf_op jit(solution)/shard_map/pallas_call | solution.py:432
  69.6 0.7 slice_subtract_fusion

commit v5 on v4

--- a/solution.py
+++ b/solution.py
@@ -258,19 +258,21 @@
 
     answer = (answer * scale[:, :CHUNK]).astype(jnp.bfloat16).astype(jnp.float32)
     answer = jnp.transpose(answer)[:RESP].astype(jnp.bfloat16)
-    gram = jnp.zeros((CAP, CAP), jnp.float32)
-    projected = jnp.zeros((RESP, CAP), jnp.float32)
+    both = jnp.zeros((CAP + RESP, CAP), jnp.float32)
     for lag in range(LAGS):
         cols = slice(lag * CHANNELS, (lag + 1) * CHANNELS)
         piece = (design[:, cols].astype(jnp.float32) * scale).astype(jnp.bfloat16)
         design[:, cols] = piece
-        gram = gram + lax.dot_general(piece, piece, NT, preferred_element_type=jnp.float32)
         fit = jnp.dot(answer, piece, preferred_element_type=jnp.float32) * (1.0 / CAP)
         cross[:, cols] = fit
-        projected = projected + lax.dot_general(
-            fit.astype(jnp.bfloat16), piece, NT, preferred_element_type=jnp.float32
+        both = both + lax.dot_general(
+            jnp.concatenate([piece, fit.astype(jnp.bfloat16)], axis=0),
+            piece,
+            NT,
+            preferred_element_type=jnp.float32,
         )
-    gram = gram * (1.0 / CAP)
+    gram = both[:CAP] * (1.0 / CAP)
+    projected = both[CAP:]
     solver[...] = gram
     bound = jnp.sqrt(jnp.sum(jnp.sum(gram * gram, axis=1, keepdims=True), axis=0, keepdims=True))
 

time: 70.4 us -> 69.9 us (level)
  no operation moved by 1% of the time
where the time goes in v5:
time: 69.9 us; the launch traced here: 69.8 us
  Pallas kernels  68.5 us (98%)
    pallas_call x1, Pallas kernels, per_device(): pl.pallas_call(functools.partial(kernel, tm, boots), out_shape=jax.ShapeD...  68.5 us

profile of v5, /device:TPU:1, one launch (start us, length us, event | category | flops | bytes accessed | tf_op | source)
XLA Modules:
  0.0 69.8 jit_solution(17032538393508624970)
XLA Ops:
  0.6 68.5 %shard_map.59 = f32[96,512]{1,0:T(8,128)S(1)} custom-call(bf16[512,1024]{1,0:T(8,128)(2,1)} %rec_hbm.1, s32[1,6]{1,0:T(1,128)} %starts_hbm.1, s32[1,6]{1,0:T(1,128)} %lengths_hbm.1, s32[8,512]{1,0:T(8,128)} %support_hbm.1), custom_call_target="tpu_custom_call" | custom-call | tf_op jit(solution)/shard_map/pallas_call | solution.py:434
  69.1 0.7 slice_subtract_fusion

commit v6 on v5

--- a/solution.py
+++ b/solution.py
@@ -243,6 +243,7 @@
     raw_rows(2)
     raw_rows(3)
     answer = jnp.dot(picks(0, SEG), rec[:, :CHUNK], preferred_element_type=jnp.float32)
+    answer = jnp.transpose(answer)[:RESP]
     arrived(halo, HALO)
     before = halo[...]
     before = jnp.where(me == 0, jnp.zeros_like(before), before)
@@ -256,8 +257,9 @@
     total = jnp.sum(power[...], axis=0)
     scale = 1.0 / jnp.sqrt(total / (SEG * tm) + EPSILON)
 
-    answer = (answer * scale[:, :CHUNK]).astype(jnp.bfloat16).astype(jnp.float32)
-    answer = jnp.transpose(answer)[:RESP].astype(jnp.bfloat16)
+    diagonal = lax.broadcasted_iota(jnp.int32, (RESP, CHUNK), 0) == lane[:RESP]
+    column = jnp.sum(jnp.where(diagonal, scale[:, :CHUNK], 0.0), axis=1, keepdims=True)
+    answer = (answer * column).astype(jnp.bfloat16)
     both = jnp.zeros((CAP + RESP, CAP), jnp.float32)
     for lag in range(LAGS):
         cols = slice(lag * CHANNELS, (lag + 1) * CHANNELS)

time: 69.9 us -> 69.9 us (level)
  no operation moved by 1% of the time
where the time goes in v6:
time: 69.9 us; the launch traced here: 69.8 us
  Pallas kernels  68.5 us (98%)
    pallas_call x1, Pallas kernels, per_device(): pl.pallas_call(functools.partial(kernel, tm, boots), out_shape=jax.ShapeD...  68.5 us

profile of v6, /device:TPU:1, one launch (start us, length us, event | category | flops | bytes accessed | tf_op | source)
XLA Modules:
  0.0 69.8 jit_solution(13698027375837974204)
XLA Ops:
  0.6 68.5 %shard_map.59 = f32[96,512]{1,0:T(8,128)S(1)} custom-call(bf16[512,1024]{1,0:T(8,128)(2,1)} %rec_hbm.1, s32[1,6]{1,0:T(1,128)} %starts_hbm.1, s32[1,6]{1,0:T(1,128)} %lengths_hbm.1, s32[8,512]{1,0:T(8,128)} %support_hbm.1), custom_call_target="tpu_custom_call" | custom-call | tf_op jit(solution)/shard_map/pallas_call | solution.py:436
  69.1 0.7 slice_subtract_fusion

commit v7 on v6

--- a/solution.py
+++ b/solution.py
@@ -147,10 +147,9 @@
 
     barrier = pltpu.get_barrier_semaphore()
 
-    @pl.loop(1, tm)
-    def _(i):
+    for o in offsets:
         pl.semaphore_signal(
-            barrier, inc=1, device_id={"tm": tm_peer(i)}, device_id_type=pl.DeviceIdType.MESH
+            barrier, inc=1, device_id={"tm": tm_at(o)}, device_id_type=pl.DeviceIdType.MESH
         )
 
     @pl.loop(1, boots)

time: 69.9 us -> 69.7 us (level)
  no operation moved by 1% of the time
where the time goes in v7:
time: 69.7 us; the launch traced here: 69.6 us
  Pallas kernels  68.3 us (98%)
    pallas_call x1, Pallas kernels, per_device(): pl.pallas_call(functools.partial(kernel, tm, boots), out_shape=jax.ShapeD...  68.3 us

profile of v7, /device:TPU:1, one launch (start us, length us, event | category | flops | bytes accessed | tf_op | source)
XLA Modules:
  0.0 69.6 jit_solution(15091635500072635004)
XLA Ops:
  0.6 68.3 %shard_map.59 = f32[96,512]{1,0:T(8,128)S(1)} custom-call(bf16[512,1024]{1,0:T(8,128)(2,1)} %rec_hbm.1, s32[1,6]{1,0:T(1,128)} %starts_hbm.1, s32[1,6]{1,0:T(1,128)} %lengths_hbm.1, s32[8,512]{1,0:T(8,128)} %support_hbm.1), custom_call_target="tpu_custom_call" | custom-call | tf_op jit(solution)/shard_map/pallas_call | solution.py:435
  69.0 0.7 slice_subtract_fusion
